TPU v7x, 512 devices: a whole 4x4x16 slice. The times are simulated.
512 devices in a mesh: row: 16 (over z), col: 8 (over x, core), rep: 4 (over y).
Axes of the slice: x: 4, y: 4, z: 16, core: 2. Of those that a mesh axis runs over, the one named last changes fastest.
Arguments:
- density: bfloat16 [6144, 6144], P('row', 'col'), as said below
- keep_square: int32 [48, 48], P('row', 'col'), may hold values 0 or 1
- keep_cube: int32 [48, 48], P('row', 'col'), may hold values 0 or 1
Outputs:
- purified: float32 [6144, 6144], P(('row', 'rep'), 'col')
Inputs may be any that keep to these rules, and one draw needn't show every extreme that they name: density is symmetric; its 128 x 128 diagonal blocks are always occupied, any other block may be zero or occupied at any distance from the diagonal.
All inputs are finite; a program needn't handle non-finite values. No bound on the sum of `keep_square` or of `keep_cube` on one device may be relied on, other than what follows from the above.
Results may differ from a plain program's by a relative error of at most 0.002.
Values may be sent and summed in bfloat16 or wider, within the bound.
No kernel may reach another device: no remote copies, remote signals or barrier semaphores. Data moves between devices by JAX's collectives and lax.ppermute only.
A program may use at most 64 MiB of HBM per device.

v0:
```python
import jax
import jax.numpy as jnp
from jax import lax
from jax.sharding import PartitionSpec as P

BLK = 128
TOP = 16384.0
TINY = 1.1754943508222875e-38
PAD = 16


def encode(piece):
    values = piece.astype(jnp.float32)
    largest = jnp.max(jnp.abs(values), axis=0, keepdims=True)
    exponent = jnp.floor(jnp.log2(jnp.maximum(largest, TINY)))
    coded = (values * jnp.exp2(-exponent) * TOP).astype(jnp.float16)
    header = jnp.broadcast_to(exponent, (PAD, piece.shape[1])).astype(jnp.float16)
    return jnp.concatenate([coded, header], axis=0)


def decode(coded, count):
    parts = coded.reshape(count, -1, coded.shape[1]).astype(jnp.float32)
    height = parts.shape[1] - PAD
    scale = jnp.exp2(parts[:, height : height + 1, :])
    values = (parts[:, :height, :] * (1.0 / TOP) * scale).astype(jnp.bfloat16)
    return values.reshape(count * height, coded.shape[1])


def local(density, keep_square, keep_cube):
    tile_rows, tile_cols = density.shape
    reps = lax.axis_size("rep")
    row_count = lax.axis_size("row")
    col_count = lax.axis_size("col")
    rep = lax.axis_index("rep")
    own = tile_rows // reps
    halves = tile_cols // tile_rows

    def section(array):
        cut = [
            lax.dynamic_slice_in_dim(array, half * tile_rows + rep * own, own, 0)
            for half in range(halves)
        ]
        return jnp.concatenate(cut, axis=0)

    right_piece = lax.dynamic_slice_in_dim(density, rep * own, own, 0)
    left_piece = section(density.T)
    left = decode(lax.all_gather(encode(left_piece), "col", axis=0, tiled=True), col_count)
    right = decode(lax.all_gather(encode(right_piece), "row", axis=0, tiled=True), row_count)

    def contract(a, b):
        return lax.dot_general(a, b, (((0,), (0,)), ((), ())), preferred_element_type=jnp.float32)

    partial = contract(right, left)
    partial = partial.reshape(halves, reps, own, tile_rows).transpose(1, 0, 2, 3)
    partial = partial.reshape(reps, halves * own, tile_rows)
    square_t = jnp.sum(lax.all_to_all(partial, "rep", 0, 0), axis=0)
    mask_rows = section(jnp.repeat(keep_square.T.astype(jnp.float32), BLK, axis=0))
    square_t = square_t * jnp.repeat(mask_rows, BLK, axis=1)
    low = decode(
        lax.all_gather(encode(square_t.astype(jnp.bfloat16)), "col", axis=0, tiled=True), col_count
    )
    cube = contract(low, right)
    mask = jnp.repeat(jnp.repeat(keep_cube.astype(jnp.float32), BLK, axis=0), BLK, axis=1)
    placed = jnp.zeros((tile_cols, tile_rows), jnp.float32)
    for half in range(halves):
        placed = lax.dynamic_update_slice_in_dim(
            placed, square_t[half * own : (half + 1) * own], half * tile_rows + rep * own, 0
        )
    total = 3.0 * placed.T - 2.0 * cube * mask
    pieces = lax.all_to_all(total.reshape(reps, own, tile_cols), "rep", 0, 0)
    return jnp.sum(pieces, axis=0)


def solution(mesh):
    return jax.shard_map(
        local,
        mesh=mesh,
        in_specs=(P("row", "col"), P("row", "col"), P("row", "col")),
        out_specs=P(("row", "rep"), "col"),
        check_vma=False,
    )
```

profile of v0, /device:TPU:1, one launch (start us, length us, event | category | flops | bytes accessed | tf_op | source)
XLA Modules:
  0.0 156.7 jit_solution(12126970050853005048)
XLA Ops:
  0.0 0.9 fusion.11
  1.0 1.0 fusion.13
  2.0 49.8 %all-gather.3 = f16[1792,768]{1,0:T(8,128)(2,1)S(1)} all-gather(f16[112,768]{1,0:T(8,128)(2,1)S(1)} %pad_maximum_fusion.3), channel_id=1, replica_groups=mesh['row'=16,'col'=8,'rep'=4] {'row'}, dimensions={0}, use_global_device_ids=true | all-gather | bytes 2924544 | tf_op jit(solution)/shard_map/all_gather | solution.py:48
  51.8 0.5 convert.3
  52.5 0.5 fusion
  53.0 2.4 %copy.12 = bf16[1536,768]{0,1:T(8,128)(2,1)} copy(bf16[1536,768]{1,0:T(8,128)(2,1)S(1)} %bitcast.59) | data formatting | bytes 4718592 | tf_op jit(solution)/shard_map/reshape | solution.py:26
  55.5 1.1 dynamic-slice_bitcast_fusion.1
  56.6 0.2 fusion.5
  57.3 0.2 copy.13
  57.5 21.3 %all-gather.4 = f16[1664,384]{1,0:T(8,128)(2,1)S(1)} all-gather(f16[208,384]{1,0:T(8,128)(2,1)S(1)} %copy.13), channel_id=1, replica_groups=mesh['row'=16,'col'=8,'rep'=4] {'col'}, dimensions={0}, use_global_device_ids=true | all-gather | bytes 1437696 | tf_op jit(solution)/shard_map/all_gather | solution.py:47
  79.1 0.2 fusion.2
  79.3 1.4 copy-done
  80.7 1.4 convolution_bitcast_fusion
  82.1 1.1 copy.14
  83.3 4.4 %all-to-all-start = ((f32[4,192,384]{2,1,0:T(8,128)}), f32[4,192,384]{2,1,0:T(8,128)}, u32[]{:S(2)}, u32[]{:S(2)}) async-start(f32[4,192,384]{2,1,0:T(8,128)} %bitcast.13), calls=%async_computation | async-start | bytes 2359296 | tf_op jit(solution)/shard_map/all_to_all | solution.py:56
  87.9 1.1 broadcast_in_dim.40
  89.0 1.6 %copy.18 = f32[384,768]{1,0:T(8,128)S(1)} copy(f32[384,768]{0,1:T(8,128)} %bitcast.66) | data formatting | bytes 2359296 | tf_op jit(solution)/shard_map/reshape | solution.py:63
  90.8 13.1 %all-to-all-done = f32[4,192,384]{2,1,0:T(8,128)} async-done(((f32[4,192,384]{2,1,0:T(8,128)}), f32[4,192,384]{2,1,0:T(8,128)}, u32[]{:S(2)}, u32[]{:S(2)}) %all-to-all-start) | async-done | bytes 1179680 | tf_op jit(solution)/shard_map/all_to_all | solution.py:56
  103.9 2.1 %reduce_sum.18 = f32[192,384]{1,0:T(8,128)} reduce(f32[4,192,384]{2,1,0:T(8,128)} %all-to-all-done, f32[]{:T(128)} %constant.15.clone.1), dimensions={0}, to_apply=%region_2.0 | reduce | flops 221184 | bytes 1474564 | tf_op jit(solution)/shard_map/reduce_sum | solution.py:56
  106.0 1.9 %copy.15 = f32[192,384]{0,1:T(8,128)} copy(f32[192,384]{1,0:T(8,128)} %reduce_sum.18) | data formatting | bytes 589824 | tf_op jit(solution)/shard_map/reduce_sum | solution.py:56
  107.9 1.1 fusion.8
  109.0 0.8 fusion.23
  110.1 0.8 pad_maximum_fusion.2
  110.9 1.7 %copy.16 = f16[208,384]{1,0:T(8,128)(2,1)} copy(f16[208,384]{0,1:T(8,128)(2,1)} %pad_maximum_fusion.2) | data formatting | bytes 319488 | tf_op jit(solution)/shard_map/concatenate | solution.py:18
  112.6 15.4 %all-gather.5 = f16[1664,384]{1,0:T(8,128)(2,1)S(1)} all-gather(f16[208,384]{1,0:T(8,128)(2,1)} %copy.16), channel_id=1, replica_groups=mesh['row'=16,'col'=8,'rep'=4] {'col'}, dimensions={0}, use_global_device_ids=true | all-gather | bytes 1437696 | tf_op jit(solution)/shard_map/all_gather | solution.py:60
  128.2 1.2 fusion.1
  129.4 1.1 broadcast_in_dim.16
  130.6 2.0 %dynamic_update_slice.6 = f32[768,384]{0,1:T(8,128)} dynamic-update-slice(f32[768,384]{0,1:T(8,128)} %broadcast_in_dim.16, f32[96,384]{0,1:T(8,128)} %get-tuple-element.10, s32[]{:T(128)S(6)} %select_n.14, s32[]{:T(128)} %constant.18.clone.1) | dynamic-update-slice | bytes 294916 | tf_op jit(solution)/shard_map/dynamic_update_slice | solution.py:66
  132.5 1.9 %dynamic_update_slice.7 = f32[768,384]{0,1:T(8,128)} dynamic-update-slice(f32[768,384]{0,1:T(8,128)} %dynamic_update_slice.6, f32[96,384]{0,1:T(8,128)} %get-tuple-element.9, s32[]{:T(128)S(6)} %select_n.15, s32[]{:T(128)} %constant.18.clone.1) | dynamic-update-slice | bytes 294916 | tf_op jit(solution)/shard_map/dynamic_update_slice | solution.py:66
  134.5 2.8 %fusion.4 = f32[384,768]{1,0:T(8,128)S(1)} fusion(f32[384,768]{1,0:T(8,128)S(1)} %copy.18, bf16[1536,384]{1,0:T(8,128)(2,1)} %bitcast.65, bf16[1536,768]{1,0:T(8,128)(2,1)S(1)} %bitcast.60, f32[768,384]{0,1:T(8,128)} %dynamic_update_slice.7), kind=kOutput, calls=%fused_computation.9 | convolution fusion | flops 907149312 | bytes 7077888 | tf_op jit(solution)/shard_map/dot_general | solution.py:51
  137.3 18.7 %all_to_all.10 = f32[4,96,768]{2,1,0:T(8,128)S(1)} all-to-all(f32[4,96,768]{2,1,0:T(8,128)S(1)} %bitcast.64), channel_id=1, replica_groups=mesh['row'=16,'col'=8,'rep'=4] {'rep'}, dimensions={0} | all-to-all | bytes 2359296 | tf_op jit(solution)/shard_map/all_to_all | solution.py:70
  155.9 0.8 reduce_sum.19
  (32 shorter events, 1.7 us)
Async XLA Ops:
  79.1 1.7 %copy-start = (bf16[1536,768]{0,1:T(8,128)(2,1)S(1)}, bf16[1536,768]{0,1:T(8,128)(2,1)}, u32[]{:S(2)}) copy-start(bf16[1536,768]{0,1:T(8,128)(2,1)} %copy.12) | copy-start | bytes 7077892
  83.2 4.4 %copy-start.1 = (s32[3,6]{1,0:T(4,128)S(1)}, s32[3,6]{1,0:T(4,128)}, u32[]{:S(2)}) copy-start(s32[3,6]{1,0:T(4,128)} %param.4) | copy-start | bytes 220
  83.2 4.5 %copy-start.2 = (s32[3,6]{1,0:T(4,128)S(1)}, s32[3,6]{1,0:T(4,128)}, u32[]{:S(2)}) copy-start(s32[3,6]{1,0:T(4,128)} %param.5) | copy-start | bytes 220
  83.3 20.7 %all-to-all-start = ((f32[4,192,384]{2,1,0:T(8,128)}), f32[4,192,384]{2,1,0:T(8,128)}, u32[]{:S(2)}, u32[]{:S(2)}) async-start(f32[4,192,384]{2,1,0:T(8,128)} %bitcast.13), calls=%async_computation | async-start | bytes 2359296 | tf_op jit(solution)/shard_map/all_to_all | solution.py:56
where the time goes:
time: 157 us
  blocking collectives  105 us (67%)
  local copies, waits for them, and re-layouts  19.1 us (12%)
  waiting for transfers between devices  13.1 us (8%)
  other arithmetic  10.5 us (7%)
  starting transfers between devices  4.39 us (3%)
  matrix products  4.17 us (3%)
    all_gather x1, blocking collectives, local(): lax.all_gather(encode(right_piece), 'row', axis=0, tiled=True)  49.8 us
    all_gather x1, blocking collectives, local(): lax.all_gather(encode(left_piece), 'col', axis=0, tiled=True)  21.3 us
    all_to_all x1, blocking collectives, local(): pieces = lax.all_to_all(total.reshape(reps, own, tile_cols), 'rep', 0, 0)  18.7 us
    all_gather x1, blocking collectives, local(): lax.all_gather(encode(square_t.astype(jnp.bfloat16)), 'col', axis=0, tile...  15.4 us
    all_to_all x1, waiting for transfers between devices, local(): square_t = jnp.sum(lax.all_to_all(partial, 'rep', 0, 0), axis=0)  13.1 us
    all_to_all x1, starting transfers between devices, local(): square_t = jnp.sum(lax.all_to_all(partial, 'rep', 0, 0), axis=0)  4.39 us
    dot_general x2, matrix products, contract(): lax.dot_general(a, b, (((0,), (0,)), ((), ())), preferred_element_type=jn...  4.17 us
    dynamic_update_slice x2, local copies, waits for them, and re-layouts, local(): lax.dynamic_update_slice_in_dim(placed, square_t[half * own:(half + 1) *...  3.9 us
  transfers between devices with their start and end apart: 1, of which 1 were waited for; matrix products, arithmetic and copies ran while one was open for 2% of the time, Pallas kernels for 0%

commit v1 on v0

--- a/solution.py
+++ b/solution.py
@@ -45,7 +45,14 @@
     right_piece = lax.dynamic_slice_in_dim(density, rep * own, own, 0)
     left_piece = section(density.T)
     left = decode(lax.all_gather(encode(left_piece), "col", axis=0, tiled=True), col_count)
-    right = decode(lax.all_gather(encode(right_piece), "row", axis=0, tiled=True), row_count)
+
+    def match_regions(local_block):
+        current_value = jax.lax.psum(1, "row")
+        base_arr = jnp.stack([local_block] * current_value)
+        new = jax.lax.all_to_all(base_arr, "row", 0, 0)
+        return jnp.concatenate(new, axis=0)
+
+    right = decode(match_regions(encode(right_piece)), row_count)
 
     def contract(a, b):
         return lax.dot_general(a, b, (((0,), (0,)), ((), ())), preferred_element_type=jnp.float32)

time: 157 us -> 223 us (1.42)
  waiting for transfers between devices: 13.1 us -> 110 us
  blocking collectives: 105 us -> 53.9 us
  starting transfers between devices: 4.39 us -> 20 us
    all_to_all x0 -> x1, waiting for transfers between devices: none -> 101 us  [match_regions(): new = jax.lax.all_to_all(base_arr, 'row', 0, 0)]
    all_gather x1 -> x0, blocking collectives: 49.8 us -> none  [local(): lax.all_gather(encode(right_piece), 'row', axis=0, tiled=True)]
    all_to_all x0 -> x1, starting transfers between devices: none -> 15.7 us  [match_regions(): new = jax.lax.all_to_all(base_arr, 'row', 0, 0)]
    all_gather x1, blocking collectives: 21.3 us -> 15 us  [local(): lax.all_gather(encode(left_piece), 'col', axis=0, tiled=True)]
    all_gather x1, blocking collectives: 15.4 us -> 20.2 us  [local(): lax.all_gather(encode(square_t.astype(jnp.bfloat16)), 'col', axis=0, tile...]
    all_to_all x1, waiting for transfers between devices: 13.1 us -> 8.84 us  [local(): square_t = jnp.sum(lax.all_to_all(partial, 'rep', 0, 0), axis=0)]
    dot_general x0 -> x1, local copies, waits for them, and re-layouts: none -> 2.44 us  [contract(): lax.dot_general(a, b, (((0,), (0,)), ((), ())), preferred_element_type=jn...]
    reshape x1 -> x0, local copies, waits for them, and re-layouts: 2.44 us -> none  [decode(): return values.reshape(count * height, coded.shape[1])]
  transfers between devices with their start and end apart: 1 -> 2, of which waited for: 1 -> 2; matrix products, arithmetic and copies ran while one was open for 2% -> 3% of each run, Pallas kernels for 0% -> 0%
where the time goes in v1:
time: 223 us; the launch traced here: 222 us
  waiting for transfers between devices  110 us (49%)
  blocking collectives  53.9 us (24%)
  local copies, waits for them, and re-layouts  20.2 us (9%)
  starting transfers between devices  20 us (9%)
  other arithmetic  11.9 us (5%)
  matrix products  5.84 us (3%)
    all_to_all x1, waiting for transfers between devices, match_regions(): new = jax.lax.all_to_all(base_arr, 'row', 0, 0)  101 us
    all_gather x1, blocking collectives, local(): lax.all_gather(encode(square_t.astype(jnp.bfloat16)), 'col', axis=0, tile...  20.2 us
    all_to_all x1, blocking collectives, local(): pieces = lax.all_to_all(total.reshape(reps, own, tile_cols), 'rep', 0, 0)  18.6 us
    all_to_all x1, starting transfers between devices, match_regions(): new = jax.lax.all_to_all(base_arr, 'row', 0, 0)  15.7 us
    all_gather x1, blocking collectives, local(): lax.all_gather(encode(left_piece), 'col', axis=0, tiled=True)  15 us
    all_to_all x1, waiting for transfers between devices, local(): square_t = jnp.sum(lax.all_to_all(partial, 'rep', 0, 0), axis=0)  8.84 us
    dot_general x2, matrix products, contract(): lax.dot_general(a, b, (((0,), (0,)), ((), ())), preferred_element_type=jn...  5.84 us
  transfers between devices with their start and end apart: 2, of which 2 were waited for; matrix products, arithmetic and copies ran while one was open for 3% of the time, Pallas kernels for 0%

profile of v1, /device:TPU:1, one launch (start us, length us, event | category | flops | bytes accessed | tf_op | source)
XLA Modules:
  0.0 222.2 jit_solution(4039199704161431435)
XLA Ops:
  0.0 0.9 fusion.11
  1.0 1.0 fusion.13
  2.0 1.7 stack.2
  3.7 15.7 %all-to-all-start = ((f16[16,112,768]{2,1,0:T(8,128)(2,1)}), f16[16,112,768]{2,1,0:T(8,128)(2,1)S(1)}, u32[]{:S(2)}, u32[]{:S(2)}) async-start(f16[16,112,768]{2,1,0:T(8,128)(2,1)} %stack.2), calls=%async_computation | async-start | bytes 5505024 | tf_op jit(solution)/shard_map/all_to_all | solution.py:52
  19.5 1.2 dynamic-slice_bitcast_fusion.1
  21.5 15.0 %all-gather.2 = f16[1664,384]{1,0:T(8,128)(2,1)S(1)} all-gather(f16[208,384]{1,0:T(8,128)(2,1)S(1)} %copy.23), channel_id=1, replica_groups=mesh['row'=16,'col'=8,'rep'=4] {'col'}, dimensions={0}, use_global_device_ids=true | all-gather | bytes 1437696 | tf_op jit(solution)/shard_map/all_gather | solution.py:47
  36.8 1.3 fusion.2
  38.1 101.4 %all-to-all-done = f16[16,112,768]{2,1,0:T(8,128)(2,1)S(1)} async-done(((f16[16,112,768]{2,1,0:T(8,128)(2,1)}), f16[16,112,768]{2,1,0:T(8,128)(2,1)S(1)}, u32[]{:S(2)}, u32[]{:S(2)}) %all-to-all-start) | async-done | bytes 2752544 | tf_op jit(solution)/shard_map/all_to_all | solution.py:52
  139.4 0.9 copy_convert_fusion
  140.4 0.6 fusion
  141.0 0.7 copy.21
  141.7 2.4 %copy.22 = bf16[768,1536]{1,0:T(8,128)(2,1)} copy(bf16[768,1536]{0,1:T(8,128)(2,1)S(1)} %bitcast.56) | data formatting | bytes 4718592 | tf_op jit(solution)/shard_map/dot_general | solution.py:58
  144.2 3.0 %convolution_bitcast_fusion = f32[4,2,96,384]{3,2,0,1:T(8,128)S(1)} fusion(bf16[2,4,96,1536]{3,2,1,0:T(8,128)(2,1)} %bitcast.63, bf16[1536,384,1,1]{1,0,3,2:T(8,128)(2,1)S(1)} %bitcast.64), kind=kOutput, calls=%fused_computation.9 | convolution fusion | flops 905969664 | bytes 4718592 | tf_op jit(solution)/shard_map/dot_general | solution.py:58
  147.3 1.1 copy.24
  148.4 4.3 %all-to-all-start.1 = ((f32[4,192,384]{2,1,0:T(8,128)}), f32[4,192,384]{2,1,0:T(8,128)}, u32[]{:S(2)}, u32[]{:S(2)}) async-start(f32[4,192,384]{2,1,0:T(8,128)} %bitcast.12), calls=%async_computation.1 | async-start | bytes 2359296 | tf_op jit(solution)/shard_map/all_to_all | solution.py:63
  152.9 1.1 broadcast_in_dim.40
  154.0 1.6 copy.28
  155.8 8.8 %all-to-all-done.1 = f32[4,192,384]{2,1,0:T(8,128)} async-done(((f32[4,192,384]{2,1,0:T(8,128)}), f32[4,192,384]{2,1,0:T(8,128)}, u32[]{:S(2)}, u32[]{:S(2)}) %all-to-all-start.1) | async-done | bytes 1179680 | tf_op jit(solution)/shard_map/all_to_all | solution.py:63
  164.7 2.1 reduce_sum.18
  166.8 1.9 copy.25
  168.6 1.1 fusion.8
  169.8 0.8 fusion.24
  170.8 0.8 pad_maximum_fusion.2
  171.6 1.7 copy.26
  173.4 20.2 %all-gather.3 = f16[1664,384]{1,0:T(8,128)(2,1)S(1)} all-gather(f16[208,384]{1,0:T(8,128)(2,1)} %copy.26), channel_id=1, replica_groups=mesh['row'=16,'col'=8,'rep'=4] {'col'}, dimensions={0}, use_global_device_ids=true | all-gather | bytes 1437696 | tf_op jit(solution)/shard_map/all_gather | solution.py:67
  193.8 1.2 fusion.1
  195.0 1.1 broadcast_in_dim.16
  196.1 2.0 dynamic_update_slice.6
  198.1 1.9 dynamic_update_slice.7
  200.0 2.8 %fusion.4 = f32[384,768]{1,0:T(8,128)S(1)} fusion(f32[384,768]{1,0:T(8,128)S(1)} %copy.28, bf16[1536,384]{1,0:T(8,128)(2,1)} %bitcast.61, bf16[1536,768]{1,0:T(8,128)(2,1)S(1)} %bitcast.57, f32[768,384]{0,1:T(8,128)} %dynamic_update_slice.7), kind=kOutput, calls=%fused_computation.10 | convolution fusion | flops 907149312 | bytes 7077888 | tf_op jit(solution)/shard_map/dot_general | solution.py:58
  202.8 18.6 %all_to_all.15 = f32[4,96,768]{2,1,0:T(8,128)S(1)} all-to-all(f32[4,96,768]{2,1,0:T(8,128)S(1)} %bitcast.60), channel_id=1, replica_groups=mesh['row'=16,'col'=8,'rep'=4] {'rep'}, dimensions={0} | all-to-all | bytes 2359296 | tf_op jit(solution)/shard_map/all_to_all | solution.py:77
  221.5 0.8 reduce_sum.19
  (34 shorter events, 2.0 us)
Async XLA Ops:
  3.7 135.7 %all-to-all-start = ((f16[16,112,768]{2,1,0:T(8,128)(2,1)}), f16[16,112,768]{2,1,0:T(8,128)(2,1)S(1)}, u32[]{:S(2)}, u32[]{:S(2)}) async-start(f16[16,112,768]{2,1,0:T(8,128)(2,1)} %stack.2), calls=%async_computation | async-start | bytes 5505024 | tf_op jit(solution)/shard_map/all_to_all | solution.py:52
  141.7 2.5 %copy-start = (bf16[8,192,384]{2,1,0:T(8,128)(2,1)S(1)}, bf16[8,192,384]{2,1,0:T(8,128)(2,1)}, u32[]{:S(2)}) copy-start(bf16[8,192,384]{2,1,0:T(8,128)(2,1)} %fusion.2) | copy-start | bytes 3538948
  147.2 5.4 %copy-start.1 = (s32[3,6]{1,0:T(4,128)S(1)}, s32[3,6]{1,0:T(4,128)}, u32[]{:S(2)}) copy-start(s32[3,6]{1,0:T(4,128)} %param.4) | copy-start | bytes 220
  147.2 5.5 %copy-start.2 = (s32[3,6]{1,0:T(4,128)S(1)}, s32[3,6]{1,0:T(4,128)}, u32[]{:S(2)}) copy-start(s32[3,6]{1,0:T(4,128)} %param.5) | copy-start | bytes 220
  148.4 16.3 %all-to-all-start.1 = ((f32[4,192,384]{2,1,0:T(8,128)}), f32[4,192,384]{2,1,0:T(8,128)}, u32[]{:S(2)}, u32[]{:S(2)}) async-start(f32[4,192,384]{2,1,0:T(8,128)} %bitcast.12), calls=%async_computation.1 | async-start | bytes 2359296 | tf_op jit(solution)/shard_map/all_to_all | solution.py:63
